TPU v7x, 256 devices: a whole 4x4x8 slice. The times are simulated.
256 devices in a mesh: quad: 8 (over x, core), leaf: 32 (over y, z).
Axes of the slice: x: 4, y: 4, z: 8, core: 2. Of those that a mesh axis runs over, the one named last changes fastest.
Arguments:
- rhs_leaf: bfloat16 [32768, 128], P('leaf'), may hold values from -6 to 6
- rhs_mid: bfloat16 [1024, 128], P('leaf'), may hold values from -6 to 6
- rhs_root: bfloat16 [1024, 128], P('leaf'), may hold values from -6 to 6
- leaf_inv: bfloat16 [16, 2, 32768, 1024], P('quad', None, 'leaf'), may hold values from -0.125 to 0.125
- leaf_couple: bfloat16 [16, 2, 4096, 1024], P('quad', None, 'leaf'), may hold values from -0.125 to 0.125
- row_lists: int32 [32, 128], P('leaf'), may hold values from 0 to 511, as said below
- leaf_sizes: int32 [32], P('leaf'), may hold values from 1 to 1024, 20480 in all
- mid_inv: bfloat16 [16, 2, 1024, 512], P('quad', None, 'leaf'), may hold values from -0.1875 to 0.1875
- mid_root: bfloat16 [16, 2, 1024, 1024], P('quad', None, 'leaf'), may hold values from -0.25 to 0.25
- root_inv: bfloat16 [16, 2, 1024, 1024], P('quad', None, 'leaf'), may hold values from -0.125 to 0.125
Outputs:
- moments_leaf: float32 [8, 32768, 128], P('quad', 'leaf')
- moments_mid: float32 [8, 1024, 128], P('quad', 'leaf')
- moments_root: float32 [8, 1024, 128], P('quad', 'leaf')
Inputs may be any that keep to these rules, and one draw needn't show every extreme that they name: `row_lists`: each row holds 128 distinct rows of the parent supernode's 512. Leaf supernode l is live on its leading leaf_sizes[l] rows; the sizes sum to 20480.
All inputs are finite; a program needn't handle non-finite values. No bound on the sum of `leaf_sizes` on one device may be relied on, other than what follows from the above.
Results may differ from a plain program's by a relative error of at most 0.019.
Values may be sent and summed in bfloat16 or wider, within the bound.
A program may use at most 64 MiB of HBM per device.

v0:
```python
import functools
import math

import jax
import jax.numpy as jnp
import numpy as np
from jax import lax
from jax.experimental import pallas as pl
from jax.experimental.pallas import tpu as pltpu
from jax.sharding import PartitionSpec as P

MESH = pl.DeviceIdType.MESH
BF16 = jnp.bfloat16
F32 = jnp.float32

MOMENTS = 8
QPOINTS = 16
PROBES = 128
LEAF = 1024
COUPLE = 128
SEP = 512
ROOT = 1024
NX, NY, NZ, NC = 4, 4, 8, 2
OWN = 32
BLOCK = OWN * NZ
SLICE = 32
SHARED = OWN + 16
CHUNK = 256
CHUNKS = LEAF // CHUNK


def nt(left, right):
    return lax.dot_general(left, right, (((1,), (1,)), ((), ())), preferred_element_type=F32)


def nn(left, right):
    return lax.dot_general(left, right, (((1,), (0,)), ((), ())), preferred_element_type=F32)


def join(with_real, with_imag):
    half = with_real.shape[0] // 2
    return jnp.concatenate(
        [with_real[:half] - with_imag[half:], with_real[half:] + with_imag[:half]], axis=0
    )


def kernel(
    rhs_leaf_h,
    rhs_mid,
    rhs_root,
    leaf_inv,
    leaf_couple,
    row_list,
    leaf_size_h,
    mid_inv,
    mid_root,
    root_inv,
    weights_h,
    out_leaf,
    out_mid,
    out_root,
    rhs_leaf,
    leaf_size,
    weights,
    inv_v,
    couple_v,
    source,
    solved_rows,
    forward,
    update,
    mid_f,
    couple_f,
    root_f,
    places,
    list_v,
    shared,
    shared_y,
    other_y,
    terms,
    terms_in,
    mid_part,
    mid_send,
    mid_recv,
    root_part,
    root_send,
    root_recv,
    back_send,
    back_recv,
    x_root,
    xmid_send,
    xmid_recv,
    x_mid,
    picked_send,
    picked,
    parts,
    own_sum,
    core_send,
    core_recv,
    chip_own,
    chip_send,
    chip_recv,
    small_send,
    small_recv,
    spread,
    rows_send,
    rows_recv,
    load_sem,
    inv_sem,
    couple_sem,
    shared_sem,
    other_sem,
    block_sem,
    relay_sem,
    pass_sem,
    terms_sem,
    mid_sem,
    root_sem,
    back_sem,
    xmid_sem,
    picked_sem,
    core_sem,
    chip_sem,
    small_sem,
    rows_sem,
    send_sem,
):
    quad, leaf = lax.axis_index("quad"), lax.axis_index("leaf")
    x, c = lax.div(quad, 2), lax.rem(quad, 2)
    y, z = lax.div(leaf, NZ), lax.rem(leaf, NZ)
    home = lax.div(z, 4)
    point = lax.rem(lax.div(z, 2), 2)
    group = 2 * lax.rem(z, 2) + c
    half = lax.rem(y, 2)
    sends = []
    counter = [0]

    def device(xx, cc, yy, zz):
        return (2 * xx + cc, NZ * yy + zz)

    def send(src, dst, recv, target):
        copy = pltpu.make_async_remote_copy(
            src_ref=src,
            dst_ref=dst,
            send_sem=send_sem.at[counter[0]],
            recv_sem=recv,
            device_id=target,
            device_id_type=MESH,
        )
        counter[0] += 1
        return copy

    def post(src, dst, recv, target):
        copy = send(src, dst, recv, target)
        copy.start()
        sends.append((None, copy))
        return copy

    def post_or_keep(src, dst, recv, cc, zz):
        mine = jnp.logical_and(cc == c, zz == z)
        copy = send(src, dst, recv, device(x, cc, y, zz))

        @pl.when(mine)
        def _():
            pltpu.make_async_copy(src, dst, recv).start()

        @pl.when(jnp.logical_not(mine))
        def _():
            copy.start()

        sends.append((mine, copy))

    def arrived(buffer, sem):
        pltpu.make_async_copy(buffer, buffer, sem).wait()

    def spread_blocks(k):
        matrix, whole, columns = pieces[k]
        for q in range(2):
            slot = lax.rem(z - 2 * (2 * c + q) + 3 + NZ, NZ)
            near = 2 * (2 * c + q) + lax.div(slot, 4)
            for cc in range(NC):
                post_or_keep(
                    matrix.at[q, cc, :, columns],
                    whole.at[cc, pl.ds(pl.multiple_of(slot * OWN, OWN), OWN), columns],
                    block_sem.at[k],
                    cc,
                    near,
                )

    first_half, second_half = pl.ds(0, ROOT // 2), pl.ds(ROOT // 2, ROOT // 2)
    pieces = (
        (mid_inv, mid_f, pl.ds(0, SEP)),
        (mid_root, couple_f, first_half),
        (mid_root, couple_f, second_half),
        (root_inv, root_f, first_half),
        (root_inv, root_f, second_half),
    )
    side = lax.rem(z, 2)
    pair = device(x, c, y, z + 1 - 2 * side)
    sibling = device(x, 1 - c, y, z)
    near_rows = pl.ds(pl.multiple_of(side * (BLOCK // 2), BLOCK // 2), BLOCK // 2)
    far_rows = pl.ds(pl.multiple_of((1 - side) * (BLOCK // 2), BLOCK // 2), BLOCK // 2)

    def relay(k):
        rows = pieces[k][1].at[c, near_rows, pieces[k][2]]
        arrived(rows, block_sem.at[k])
        return [
            post(rows, rows, relay_sem.at[k], pair),
            post(rows, rows, pass_sem.at[k, 0], sibling),
        ]

    def pass_far(k, copies):
        copies[0].wait_recv()
        rows = pieces[k][1].at[c, far_rows, pieces[k][2]]
        copies.append(post(rows, rows, pass_sem.at[k, 1], sibling))

    def complete(copies):
        copies[1].wait_recv()
        copies[2].wait_recv()

    loads = [
        pltpu.make_async_copy(leaf_size_h, leaf_size, load_sem.at[0]),
        pltpu.make_async_copy(rhs_leaf_h, rhs_leaf, load_sem.at[1]),
        pltpu.make_async_copy(weights_h, weights, load_sem.at[2]),
        pltpu.make_async_copy(row_list, list_v, load_sem.at[3]),
    ]
    for load in loads:
        load.start()
    mid_load = pltpu.make_async_copy(rhs_mid, shared.at[pl.ds(0, OWN)], load_sem.at[4])
    root_load = pltpu.make_async_copy(rhs_root, shared.at[pl.ds(0, OWN)], load_sem.at[4])

    @pl.when(c == 0)
    def _():
        mid_load.start()

    @pl.when(c == 1)
    def _():
        root_load.start()

    for i in range(4):
        block = (i // 2, i % 2)
        pltpu.make_async_copy(leaf_inv.at[block], inv_v.at[block], inv_sem.at[i]).start()
    couple_load = pltpu.make_async_copy(leaf_couple, couple_v, couple_sem)
    couple_load.start()

    barrier = pltpu.get_barrier_semaphore()
    mates = []
    for i in range(1, NC * NZ):
        place = lax.rem(c * NZ + z + i, NC * NZ)
        mates.append(device(x, lax.div(place, NZ), y, lax.rem(place, NZ)))
    y_mates = [device(x, c, lax.rem(y + d, NY), z) for d in range(1, NY)]
    x_mates = [device(lax.rem(x + d, NX), c, y, z) for d in range(1, NX)]
    for mate in mates + y_mates + x_mates:
        pl.semaphore_signal(barrier, inc=1, device_id=mate, device_id_type=MESH)

    for load in loads:
        load.wait()
    mid_load.wait()
    size = leaf_size[0]
    listed = jnp.broadcast_to(list_v[...], (16, COUPLE))
    high = lax.div(listed, 16)
    low = listed - 16 * high
    first_row = lax.broadcasted_iota(jnp.int32, (16, COUPLE), 0) == 0
    shared[OWN:SHARED, :] = jnp.where(first_row, high, low).astype(F32).astype(BF16)
    row_live = lax.broadcasted_iota(jnp.int32, (LEAF, PROBES), 0) < size
    source[...] = jnp.where(row_live, rhs_leaf[...].astype(F32), 0.0).astype(BF16)

    def forward_step(i, carry):
        q, a = lax.div(i, 2), lax.rem(i, 2)
        arrived(inv_v.at[q, a], inv_sem.at[i])
        product = nn(inv_v[q, a], source[...])
        live = lax.broadcasted_iota(jnp.int32, product.shape, 0) < size
        solved_rows[q, :, pl.ds(pl.multiple_of(a * PROBES, PROBES), PROBES)] = jnp.where(
            live, product, 0.0
        ).astype(BF16)
        return carry

    def couple_step(q):
        with_real = nn(couple_v[q, 0], solved_rows[q])
        with_imag = nn(couple_v[q, 1], solved_rows[q])
        terms[q, 0] = (with_real[:, :PROBES] - with_imag[:, PROBES:]).T.astype(BF16)
        terms[q, 1] = (with_real[:, PROBES:] + with_imag[:, :PROBES]).T.astype(BF16)

    def terms_out(q):
        for t in (2 * q, 2 * q + 1):
            for cc in range(NC):
                pg = 2 * (t % 2) + cc
                post_or_keep(
                    terms.at[q, :, pl.ds(pg * SLICE, SLICE), :],
                    terms_in.at[:, :, pl.ds(pl.multiple_of(z * COUPLE, COUPLE), COUPLE)],
                    terms_sem,
                    cc,
                    4 * c + t,
                )

    lax.fori_loop(0, 4, forward_step, 0)
    couple_load.wait()
    couple_step(0)
    couple_step(1)
    pl.semaphore_wait(barrier, len(mates) + len(y_mates) + len(x_mates))

    spread_blocks(1)
    terms_out(0)
    terms_out(1)
    spread_blocks(2)
    spread_blocks(0)
    pltpu.make_async_copy(shared, shared_y.at[z], shared_sem).start()
    for d in range(1, NZ):
        post(shared, shared_y.at[z], shared_sem, device(x, c, y, lax.rem(z + d, NZ)))

    couple_copies = [relay(1), relay(2)]
    spread_blocks(3)
    spread_blocks(4)
    mid_copies = relay(0)
    arrived(shared_y, shared_sem)
    other_copy = post(shared_y.at[:, pl.ds(0, OWN)], other_y, other_sem, sibling)
    for l in range(NZ):
        sep_row = lax.broadcasted_iota(jnp.int32, (SEP, COUPLE), 0)
        codes = shared_y[l, OWN:SHARED, :].astype(F32)
        listed = (16.0 * codes[0:1] + codes[1:2]).astype(jnp.int32)
        places[:, l * COUPLE : (l + 1) * COUPLE] = (
            jnp.where(sep_row == listed, 1.0, 0.0).astype(BF16)
        )
    chosen = jnp.where(
        lax.broadcasted_iota(jnp.int32, (SLICE, PROBES), 1)
        == lax.broadcasted_iota(jnp.int32, (SLICE, PROBES), 0) + group * SLICE,
        1.0,
        0.0,
    ).astype(BF16)
    other_copy.wait_recv()
    mine_t = nt(chosen, shared_y[:, 0:OWN, :].reshape(BLOCK, PROBES))
    other_t = nt(chosen, other_y[...].reshape(BLOCK, PROBES))
    rhs_mid_t = jnp.where(c == 0, mine_t, other_t)
    rhs_root_t = jnp.where(c == 0, other_t, mine_t)

    for q in range(2):
        forward[q] = solved_rows[q].T

    half_rows = pl.ds(pl.multiple_of(half * BLOCK, BLOCK), BLOCK)
    block_rows = pl.ds(pl.multiple_of(y * BLOCK, BLOCK), BLOCK)
    partner = device(x, c, y + 1 - 2 * half, z)
    arrived(terms_in, terms_sem)
    mid_part[...] = -nt(terms_in[...].reshape(2 * SLICE, NZ * COUPLE), places[...])
    mid_part[0:SLICE, half_rows] += rhs_mid_t
    mid_send[...] = mid_part[...].astype(BF16)
    mid_copy = post(mid_send, mid_recv, mid_sem, partner)
    pass_far(1, couple_copies[0])
    pass_far(2, couple_copies[1])
    pass_far(0, mid_copies)
    mid_copy.wait_recv()
    residual_mid = (mid_part[...] + mid_recv[...].astype(F32)).astype(BF16)
    complete(mid_copies)
    forward_mid = join(nt(residual_mid, mid_f[0]), nt(residual_mid, mid_f[1])).astype(BF16)

    def sum_over_y(part, out, into, sem):
        out[...] = part[...].astype(BF16)
        return [
            post(out, into.at[d], sem.at[d], y_mates[d]) for d in range(NY - 1)
        ]

    def total(part, into, copies):
        for copy in copies:
            copy.wait_recv()
        summed = part[...]
        for d in range(NY - 1):
            summed = summed + into[d].astype(F32)
        return summed.astype(BF16)

    root_copies = [relay(3)]
    complete(couple_copies[0])
    complete(couple_copies[1])
    root_part[...] = -join(nn(forward_mid, couple_f[0]), nn(forward_mid, couple_f[1]))
    root_part[0:SLICE, block_rows] += rhs_root_t
    copies = sum_over_y(root_part, root_send, root_recv, root_sem)
    root_copies.append(relay(4))
    pass_far(3, root_copies[0])
    pass_far(4, root_copies[1])
    residual_root = total(root_part, root_recv, copies)
    complete(root_copies[0])
    complete(root_copies[1])
    forward_root = join(nt(residual_root, root_f[0]), nt(residual_root, root_f[1])).astype(BF16)
    root_part[...] = join(nn(forward_root, root_f[0]), nn(forward_root, root_f[1]))
    copies = sum_over_y(root_part, back_send, back_recv, back_sem)
    x_root[...] = total(root_part, back_recv, copies)

    from_root = join(nt(x_root[...], couple_f[0]), nt(x_root[...], couple_f[1]))
    update_mid = (forward_mid.astype(F32) - from_root).astype(BF16)
    mid_part[...] = join(nn(update_mid, mid_f[0]), nn(update_mid, mid_f[1]))
    xmid_send[...] = mid_part[...].astype(BF16)
    xmid_copy = post(xmid_send, xmid_recv, xmid_sem, partner)
    xmid_copy.wait_recv()
    x_mid[...] = (mid_part[...] + xmid_recv[...].astype(F32)).astype(BF16)
    picked_send[...] = nn(x_mid[...], places[...]).astype(BF16).reshape(2, SLICE, NZ * COUPLE)
    for d in range(NZ):
        zl = lax.rem(z + d, NZ)
        post_or_keep(
            picked_send.at[:, :, pl.ds(pl.multiple_of(zl * COUPLE, COUPLE), COUPLE)],
            picked.at[point, :, pl.ds(pl.multiple_of(group * SLICE, SLICE), SLICE), :],
            picked_sem,
            home,
            zl,
        )

    small_send[:, 0:BLOCK] = x_root[:, block_rows]
    small_send[:, BLOCK:] = x_mid[:, half_rows]
    small_copies = [
        post(small_send, small_recv.at[d], small_sem.at[d], x_mates[d]) for d in range(NX - 1)
    ]

    arrived(picked, picked_sem)
    for q in range(2):
        picked_q = picked[q].reshape(2 * PROBES, COUPLE)
        for n in range(2):
            columns = slice(n * 512, (n + 1) * 512)
            change = join(nn(picked_q, couple_v[q, 0, :, columns]), nn(picked_q, couple_v[q, 1, :, columns]))
            live = lax.broadcasted_iota(jnp.int32, change.shape, 1) + n * 512 < size
            update[q, :, columns] = jnp.where(
                live, forward[q, :, columns].astype(F32) - change, 0.0
            ).astype(BF16)

    first = 2 * quad

    core_base, chip_base = counter[0], counter[0] + CHUNKS
    counter[0] += CHUNKS + CHUNKS * (NX - 1)

    def core_copy(i):
        return pltpu.make_async_remote_copy(
            src_ref=core_send.at[i],
            dst_ref=core_recv.at[i],
            send_sem=send_sem.at[core_base + i],
            recv_sem=core_sem.at[i],
            device_id=sibling,
            device_id_type=MESH,
        )

    def chip_copy(i, d):
        return pltpu.make_async_remote_copy(
            src_ref=chip_send.at[i, d],
            dst_ref=chip_recv.at[i, d],
            send_sem=send_sem.at[chip_base + i * (NX - 1) + d],
            recv_sem=chip_sem.at[i, d],
            device_id=x_mates[d],
            device_id_type=MESH,
        )

    def leaf_step(i):
        columns = pl.ds(pl.multiple_of(i * CHUNK, CHUNK), CHUNK)
        for q in range(2):
            solved = join(
                nn(update[q], inv_v[q, 0, :, columns]), nn(update[q], inv_v[q, 1, :, columns])
            )
            live = lax.broadcasted_iota(jnp.int32, solved.shape, 1) + i * CHUNK < size
            parts[pl.ds(2 * q * PROBES, 2 * PROBES), :] = jnp.where(live, solved, 0.0)

        def moment(k):
            total_k = None
            for q in range(2):
                for a in range(2):
                    row = (2 * q + a) * PROBES
                    term = weights[first + q, 2 * k + a] * parts[row : row + PROBES, :]
                    total_k = term if total_k is None else total_k + term
            return total_k

        for xx in range(NX):
            core_send[i, xx] = moment(2 * xx + 1 - c).astype(BF16)
            own_sum[i, xx] = moment(2 * xx + c)
        core_copy(i).start()

    def chip_step(i):
        core_copy(i).wait_recv()
        chip_own[i] = own_sum[i, x] + core_recv[i, x].astype(F32)
        for d in range(NX - 1):
            xx = lax.rem(x + d + 1, NX)
            chip_send[i, d] = (own_sum[i, xx] + core_recv[i, xx].astype(F32)).astype(BF16)
            chip_copy(i, d).start()

    def tail_step(i, carry):
        leaf_step(i)

        @pl.when(i > 0)
        def _():
            chip_step(i - 1)

        return carry

    lax.fori_loop(0, CHUNKS, tail_step, 0)
    chip_step(CHUNKS - 1)

    for copy in small_copies:
        copy.wait_recv()
    hosted = lax.div(z, 2)
    pieces = [small_send[...].astype(F32)] + [small_recv[d].astype(F32) for d in range(NX - 1)]
    spread[...] = jnp.zeros_like(spread)
    for cc in range(NC):
        total_k = None
        for d in range(NX):
            point_d = 4 * lax.rem(x + NX - d, NX) + hosted
            real = weights[point_d, 2 * (2 * x + cc)] * pieces[d][0:SLICE]
            imag = weights[point_d, 2 * (2 * x + cc) + 1] * pieces[d][SLICE:]
            total_k = real + imag if total_k is None else total_k + (real + imag)
        spread[pl.ds(pl.multiple_of(group * SLICE, SLICE), SLICE), :] = total_k
        rows_send[cc] = spread[...].T.astype(BF16).reshape(2, BLOCK, PROBES)
    for i in range(NC * NZ):
        place = lax.rem(c * NZ + z + i, NC * NZ)
        cc, zz = lax.div(place, NZ), lax.rem(place, NZ)
        src = rows_send.at[cc, :, pl.ds(pl.multiple_of(zz * OWN, OWN), OWN), :]
        dst = rows_recv.at[i]
        if i == 0:
            pltpu.make_async_copy(src, dst, rows_sem).start()
        else:
            post(src, dst, rows_sem, device(x, cc, y, zz))
    arrived(rows_recv, rows_sem)
    gathered = rows_recv[0].astype(F32)
    for i in range(1, NC * NZ):
        gathered = gathered + rows_recv[i].astype(F32)
    out_root[0] = gathered[0]
    out_mid[0] = gathered[1]

    for i in range(CHUNKS):
        result = chip_own[i]
        for d in range(NX - 1):
            chip_copy(i, d).wait_recv()
            result = result + chip_recv[i, d].astype(F32)
        out_leaf[0, i * CHUNK : (i + 1) * CHUNK, :] = result.T

    for mine, copy in sends:
        if mine is None:
            copy.wait_send()
        else:

            @pl.when(jnp.logical_not(mine))
            def _():
                copy.wait_send()

    for i in range(CHUNKS):
        core_copy(i).wait_send()
        for d in range(NX - 1):
            chip_copy(i, d).wait_send()


def deliver(leaf, mid, root, out_leaf, out_mid, out_root):
    out_leaf[...] = leaf[...]
    out_mid[...] = mid[...]
    out_root[...] = root[...]


def weight_table():
    table = np.zeros((QPOINTS, 2 * MOMENTS), np.float32)
    for q in range(QPOINTS):
        for k in range(MOMENTS):
            angle = 2.0 * math.pi * (q + 0.5) / QPOINTS * (k + 1)
            table[q, 2 * k] = 4.0 / QPOINTS * math.cos(angle)
            table[q, 2 * k + 1] = -4.0 / QPOINTS * math.sin(angle)
    return jnp.asarray(table)


def body(*arrays):
    vmem = pl.BlockSpec(memory_space=pltpu.VMEM)
    hbm = pl.BlockSpec(memory_space=pltpu.HBM)
    in_specs = [hbm] * 11
    out_shape = [
        jax.ShapeDtypeStruct((1, LEAF, PROBES), F32),
        jax.ShapeDtypeStruct((1, OWN, PROBES), F32),
        jax.ShapeDtypeStruct((1, OWN, PROBES), F32),
    ]
    cols = 2 * SLICE
    dma = pltpu.SemaphoreType.DMA
    scratch = [
        pltpu.VMEM((LEAF, PROBES), BF16),
        pltpu.SMEM((1,), jnp.int32),
        pltpu.SMEM((QPOINTS, 2 * MOMENTS), F32),
        pltpu.VMEM((2, 2, LEAF, LEAF), BF16),
        pltpu.VMEM((2, 2, COUPLE, LEAF), BF16),
        pltpu.VMEM((LEAF, PROBES), BF16),
        pltpu.VMEM((2, LEAF, 2 * PROBES), BF16),
        pltpu.VMEM((2, 2 * PROBES, LEAF), BF16),
        pltpu.VMEM((2, 2 * PROBES, LEAF), BF16),
        pltpu.VMEM((2, BLOCK, SEP), BF16),
        pltpu.VMEM((2, BLOCK, ROOT), BF16),
        pltpu.VMEM((2, BLOCK, ROOT), BF16),
        pltpu.VMEM((SEP, NZ * COUPLE), BF16),
        pltpu.VMEM((1, COUPLE), jnp.int32),
        pltpu.VMEM((SHARED, PROBES), BF16),
        pltpu.VMEM((NZ, SHARED, PROBES), BF16),
        pltpu.VMEM((NZ, OWN, PROBES), BF16),
        pltpu.VMEM((2, 2, PROBES, COUPLE), BF16),
        pltpu.VMEM((2, SLICE, NZ * COUPLE), BF16),
        pltpu.VMEM((cols, SEP), F32),
        pltpu.VMEM((cols, SEP), BF16),
        pltpu.VMEM((cols, SEP), BF16),
        pltpu.VMEM((cols, ROOT), F32),
        pltpu.VMEM((cols, ROOT), BF16),
        pltpu.VMEM((NY - 1, cols, ROOT), BF16),
        pltpu.VMEM((cols, ROOT), BF16),
        pltpu.VMEM((NY - 1, cols, ROOT), BF16),
        pltpu.VMEM((cols, ROOT), BF16),
        pltpu.VMEM((cols, SEP), BF16),
        pltpu.VMEM((cols, SEP), BF16),
        pltpu.VMEM((cols, SEP), BF16),
        pltpu.VMEM((2, SLICE, NZ * COUPLE), BF16),
        pltpu.VMEM((2, 2, PROBES, COUPLE), BF16),
        pltpu.VMEM((4 * PROBES, CHUNK), F32),
        pltpu.VMEM((CHUNKS, NX, PROBES, CHUNK), F32),
        pltpu.VMEM((CHUNKS, NX, PROBES, CHUNK), BF16),
        pltpu.VMEM((CHUNKS, NX, PROBES, CHUNK), BF16),
        pltpu.VMEM((CHUNKS, PROBES, CHUNK), F32),
        pltpu.VMEM((CHUNKS, NX - 1, PROBES, CHUNK), BF16),
        pltpu.VMEM((CHUNKS, NX - 1, PROBES, CHUNK), BF16),
        pltpu.VMEM((cols, 2 * BLOCK), BF16),
        pltpu.VMEM((NX - 1, cols, 2 * BLOCK), BF16),
        pltpu.VMEM((PROBES, 2 * BLOCK), F32),
        pltpu.VMEM((NC, 2, BLOCK, PROBES), BF16),
        pltpu.VMEM((NC * NZ, 2, OWN, PROBES), BF16),
        dma((5,)),
        dma((4,)),
        dma,
        dma,
        dma,
        dma((5,)),
        dma((5,)),
        dma((5, 2)),
        dma,
        dma,
        dma((NY - 1,)),
        dma((NY - 1,)),
        dma,
        dma,
        dma((CHUNKS,)),
        dma((CHUNKS, NX - 1)),
        dma((NX - 1,)),
        dma,
        dma((128,)),
    ]
    results = pl.pallas_call(
        kernel,
        out_shape=out_shape,
        in_specs=in_specs,
        out_specs=[vmem, vmem, vmem],
        scratch_shapes=scratch,
        compiler_params=pltpu.CompilerParams(
            collective_id=0, has_side_effects=True, vmem_limit_bytes=56 * 2**20
        ),
    )(*arrays, weight_table())
    return tuple(
        pl.pallas_call(
            deliver,
            out_shape=out_shape,
            in_specs=[vmem] * 3,
            out_specs=[vmem] * 3,
        )(*results)
    )


def solution(mesh):
    in_specs = (
        P("leaf", None),
        P("leaf", None),
        P("leaf", None),
        P("quad", None, "leaf", None),
        P("quad", None, "leaf", None),
        P("leaf", None),
        P("leaf"),
        P("quad", None, "leaf", None),
        P("quad", None, "leaf", None),
        P("quad", None, "leaf", None),
    )
    out_specs = (P("quad", "leaf", None), P("quad", "leaf", None), P("quad", "leaf", None))
    return jax.shard_map(body, mesh=mesh, in_specs=in_specs, out_specs=out_specs, check_vma=False)
```

profile of v0, /device:TPU:1, one launch (start us, length us, event | category | flops | bytes accessed | tf_op | source)
XLA Modules:
  0.0 87.9 jit_solution(12152388397377755216)
XLA Ops:
  1.3 84.7 %shard_map.130 = (f32[1,1024,128]{2,1,0:T(8,128)}, f32[1,32,128]{2,1,0:T(8,128)}, f32[1,32,128]{2,1,0:T(8,128)}) custom-call(bf16[1024,128]{1,0:T(8,128)(2,1)} %rhs_leaf_h.1, bf16[32,128]{1,0:T(8,128)(2,1)} %rhs_mid.1, bf16[32,128]{1,0:T(8,128)(2,1)} %rhs_root.1, bf16[2,2,1024,1024]{3,2,1,0:T(8,128)(2,1)} %leaf_inv.1, bf16[2,2,128,1024]{3,2,1,0:T(8,128)(2,1)} %leaf_couple.1, ...), custom_call_target="tpu_custom_call" | custom-call | tf_op jit(solution)/shard_map/pallas_call | solution.py:633
  86.0 1.9 %shard_map.131 = (f32[1,1024,128]{2,1,0:T(8,128)}, f32[1,32,128]{2,1,0:T(8,128)}, f32[1,32,128]{2,1,0:T(8,128)}) custom-call(f32[1,1024,128]{2,1,0:T(8,128)} %get-tuple-element.6.leaf, f32[1,32,128]{2,1,0:T(8,128)} %get-tuple-element.7.mid, f32[1,32,128]{2,1,0:T(8,128)} %get-tuple-element.8.root), custom_call_target="tpu_custom_call" | custom-call | tf_op jit(solution)/shard_map/pallas_call | solution.py:644
where the time goes:
time: 88 us; the launch traced here: 87.9 us
  Pallas kernels  86.6 us (98%)
  between operations  1.29 us (1%)
    pallas_call x1, Pallas kernels, body(): pl.pallas_call(kernel, out_shape=out_shape, in_specs=in_specs, out_specs=...  84.7 us
    pallas_call x1, Pallas kernels, body(): pl.pallas_call(deliver, out_shape=out_shape, in_specs=[vmem] * 3, out_spe...  1.89 us

commit v1 on v0

--- a/solution.py
+++ b/solution.py
@@ -468,7 +468,7 @@
     def chip_step(i):
         core_copy(i).wait_recv()
         chip_own[i] = own_sum[i, x] + core_recv[i, x].astype(F32)
-        for d in range(NX - 1):
+        for d in (1, 0, 2):
             xx = lax.rem(x + d + 1, NX)
             chip_send[i, d] = (own_sum[i, xx] + core_recv[i, xx].astype(F32)).astype(BF16)
             chip_copy(i, d).start()

time: 88 us -> 87.7 us (level)
  no operation moved by 1% of the time
where the time goes in v1:
time: 87.7 us; the launch traced here: 87.6 us
  Pallas kernels  86.3 us (98%)
  between operations  1.29 us (1%)
    pallas_call x1, Pallas kernels, body(): pl.pallas_call(kernel, out_shape=out_shape, in_specs=in_specs, out_specs=...  84.4 us
    pallas_call x1, Pallas kernels, body(): pl.pallas_call(deliver, out_shape=out_shape, in_specs=[vmem] * 3, out_spe...  1.89 us

profile of v1, /device:TPU:1, one launch (start us, length us, event | category | flops | bytes accessed | tf_op | source)
XLA Modules:
  0.0 87.6 jit_solution(10408860526830543238)
XLA Ops:
  1.3 84.4 %shard_map.130 = (f32[1,1024,128]{2,1,0:T(8,128)}, f32[1,32,128]{2,1,0:T(8,128)}, f32[1,32,128]{2,1,0:T(8,128)}) custom-call(bf16[1024,128]{1,0:T(8,128)(2,1)} %rhs_leaf_h.1, bf16[32,128]{1,0:T(8,128)(2,1)} %rhs_mid.1, bf16[32,128]{1,0:T(8,128)(2,1)} %rhs_root.1, bf16[2,2,1024,1024]{3,2,1,0:T(8,128)(2,1)} %leaf_inv.1, bf16[2,2,128,1024]{3,2,1,0:T(8,128)(2,1)} %leaf_couple.1, ...), custom_call_target="tpu_custom_call" | custom-call | tf_op jit(solution)/shard_map/pallas_call | solution.py:633
  85.7 1.9 %shard_map.131 = (f32[1,1024,128]{2,1,0:T(8,128)}, f32[1,32,128]{2,1,0:T(8,128)}, f32[1,32,128]{2,1,0:T(8,128)}) custom-call(f32[1,1024,128]{2,1,0:T(8,128)} %get-tuple-element.6.leaf, f32[1,32,128]{2,1,0:T(8,128)} %get-tuple-element.7.mid, f32[1,32,128]{2,1,0:T(8,128)} %get-tuple-element.8.root), custom_call_target="tpu_custom_call" | custom-call | tf_op jit(solution)/shard_map/pallas_call | solution.py:644
